TPU v7x, 512 devices: a whole 4x4x16 slice. The times are simulated.
512 devices in a mesh: dp: 16 (over x, y), tile: 32 (over z, core).
Axes of the slice: x: 4, y: 4, z: 16, core: 2. Of those that a mesh axis runs over, the one named last changes fastest.
Arguments:
- calibration: bfloat16 [2048, 32768], P('dp', 'tile'), may hold values from -72 to 72
- sketch: bfloat16 [32768, 256], P('tile'), may hold values from -6 to 6
- weights: bfloat16 [16384, 32768], P(('dp', 'tile')), may hold values from -6 to 6
- tile_ranks: int32 [16, 32], P('dp', 'tile'), may hold values from 32 to 256
Outputs:
- basis_factor: bfloat16 [16384, 8192], P(('dp', 'tile'))
- coefficients: bfloat16 [4096, 32768], P('dp', 'tile')
All inputs are finite; a program needn't handle non-finite values.
Results may differ from a plain program's by a relative error of at most 0.007.
Values may be sent and summed in bfloat16 or wider, within the bound.
No kernel may reach another device: no remote copies, remote signals or barrier semaphores. Data moves between devices by JAX's collectives and lax.ppermute only.
A program may use at most 128 MiB of HBM per device.

v0:
```python
import math

import jax
import jax.numpy as jnp
from jax import lax
from jax.sharding import PartitionSpec as P

DAMPING = 0.1


def factor(gram):
    width = gram.shape[0]
    mean_diag = jnp.mean(jnp.diagonal(gram))
    held = gram + DAMPING * mean_diag * jnp.eye(width, dtype=jnp.float32)
    return jnp.linalg.cholesky(held)


def compress(tile_block, sketched, tile_rank):
    width = tile_block.shape[0]
    columns = jnp.arange(sketched.shape[1], dtype=jnp.int32)
    kept_cols = columns < tile_rank
    masked = sketched * kept_cols.astype(jnp.bfloat16)
    range_rows = jnp.dot(tile_block, masked, preferred_element_type=jnp.float32)
    inner_gram = lax.dot_general(
        range_rows, range_rows, (((0,), (0,)), ((), ())), precision=lax.Precision.HIGHEST
    )
    inner_gram = inner_gram + jnp.diag(1.0 - kept_cols.astype(jnp.float32))
    inner_lower = jnp.linalg.cholesky(inner_gram)
    basis_t = jax.scipy.linalg.solve_triangular(inner_lower, range_rows.T, lower=True) * math.sqrt(
        width
    )
    basis_bf = basis_t.astype(jnp.bfloat16)
    coeffs = jnp.dot(basis_bf, tile_block, preferred_element_type=jnp.float32) / math.sqrt(width)
    return (basis_bf.T, coeffs.astype(jnp.bfloat16))


def self_gram(rows_block):
    return lax.dot_general(
        rows_block, rows_block, (((0,), (0,)), ((), ())), preferred_element_type=jnp.float32
    )


def local(calibration, sketch, weights, tile_ranks):
    partial_value = self_gram(calibration)
    gram = lax.psum(partial_value, "dp")
    whitener = factor(gram)
    sketched = jnp.dot(
        whitener, sketch.astype(jnp.float32), precision=lax.Precision.HIGHEST
    ).astype(jnp.bfloat16)
    tile_block = lax.all_to_all(weights, "tile", split_axis=1, concat_axis=0, tiled=True)
    basis_rows, coeffs = compress(tile_block, sketched, tile_ranks[0, 0])
    served = lax.all_to_all(basis_rows, "tile", split_axis=0, concat_axis=1, tiled=True)
    return (served, coeffs)


def solution(mesh):
    placed = (P("dp", "tile"), P("tile", None), P(("dp", "tile"), None), P("dp", "tile"))
    return jax.shard_map(
        local,
        mesh=mesh,
        in_specs=placed,
        out_specs=(P(("dp", "tile"), None), P("dp", "tile")),
        check_vma=False,
    )
```

profile of v0, /device:TPU:1, one launch (start us, length us, event | category | flops | bytes accessed | tf_op | source)
XLA Modules:
  0.0 530.7 jit_solution(16582082554035921322)
XLA Ops:
  7.2 3.9 fusion.59
  12.8 16.8 %all-to-all-start = ((bf16[32,32,1024]{2,0,1:T(8,128)(2,1)}), bf16[32,32,1024]{2,0,1:T(8,128)(2,1)S(1)}, u32[]{:S(2)}, u32[]{:S(2)}) async-start(bf16[32,32,1024]{2,0,1:T(8,128)(2,1)} %bitcast.107), calls=%async_computation | async-start | bytes 4194304 | tf_op jit(solution)/shard_map/all_to_all | solution.py:50
  30.8 119.9 %all-reduce.4.cloned.1.call-done = f32[1024,1024]{0,1:T(8,128)} async-done(((f32[1024,1024]{0,1:T(8,128)}), f32[1024,1024]{0,1:T(8,128)}) %all-reduce.4.cloned.1.call-update) | async-done | bytes 4194320 | tf_op jit(solution)/shard_map/psum | solution.py:45
  150.8 17.3 %gather_fusion = f32[1024]{0:T(1024)S(1)} fusion(f32[1024,1024]{0,1:T(8,128)} %all-reduce.4.cloned.1.call-done, s32[1024]{0:T(1024)S(1)} %bitcast.104), kind=kCustom, calls=%fused_computation | custom fusion | bytes 16384 | tf_op jit(solution)/shard_map/jit(diagonal)/cond/branch_0_fun/gather | solution.py:13
  169.3 4.8 select_add_fusion
  174.1 5.8 %copy.66 = f32[1024,1024]{1,0:T(8,128)} copy(f32[1024,1024]{0,1:T(8,128)} %select_add_fusion) | data formatting | bytes 8388608 | tf_op jit(solution)/shard_map/add | solution.py:14
  180.0 4.5 fusion
  186.4 11.7 %cholesky.248 = f32[128,128]{1,0:T(8,128)S(1)} custom-call(f32[128,128]{1,0:T(8,128)S(1)} %cholesky.647), custom_call_target="Cholesky" | custom-call | tf_op jit(solution)/shard_map/jit(cholesky)/cholesky | solution.py:15
  200.7 9.8 %custom-call.67 = f32[1,128,128]{1,2,0:T(8,128)S(1)} custom-call(f32[1,128,128]{2,1,0:T(8,128)S(1)} %get-tuple-element.38), custom_call_target="InvertDiagBlocksLowerTriangular" | custom-call | tf_op jit(solution)/shard_map/jit(cholesky)/cholesky | solution.py:15
  214.6 11.9 %cholesky.271 = f32[128,128]{1,0:T(8,128)S(1)} custom-call(f32[128,128]{1,0:T(8,128)S(1)} %cholesky.651), custom_call_target="Cholesky" | custom-call | tf_op jit(solution)/shard_map/jit(cholesky)/cholesky | solution.py:15
  226.6 9.8 %custom-call.68 = f32[1,128,128]{1,2,0:T(8,128)S(1)} custom-call(f32[1,128,128]{2,1,0:T(8,128)S(1)} %get-tuple-element.36), custom_call_target="InvertDiagBlocksLowerTriangular" | custom-call | tf_op jit(solution)/shard_map/jit(cholesky)/cholesky | solution.py:15
  242.9 11.7 %cholesky.298 = f32[128,128]{1,0:T(8,128)S(1)} custom-call(f32[128,128]{1,0:T(8,128)S(1)} %cholesky.656), custom_call_target="Cholesky" | custom-call | tf_op jit(solution)/shard_map/jit(cholesky)/cholesky | solution.py:15
  254.8 9.8 %custom-call.69 = f32[1,128,128]{1,2,0:T(8,128)S(1)} custom-call(f32[1,128,128]{2,1,0:T(8,128)S(1)} %get-tuple-element.34), custom_call_target="InvertDiagBlocksLowerTriangular" | custom-call | tf_op jit(solution)/shard_map/jit(cholesky)/cholesky | solution.py:15
  266.5 3.4 convolution_subtract_fusion.3
  269.9 11.7 %cholesky.537 = f32[128,128]{1,0:T(8,128)S(1)} custom-call(f32[128,128]{1,0:T(8,128)S(1)} %cholesky.661), custom_call_target="Cholesky" | custom-call | tf_op jit(solution)/shard_map/jit(cholesky)/cholesky | solution.py:15
  281.7 9.8 %custom-call.70 = f32[1,128,128]{1,2,0:T(8,128)S(1)} custom-call(f32[1,128,128]{2,1,0:T(8,128)S(1)} %get-tuple-element.32), custom_call_target="InvertDiagBlocksLowerTriangular" | custom-call | tf_op jit(solution)/shard_map/jit(cholesky)/cholesky | solution.py:15
  293.3 3.2 convolution_subtract_fusion.4
  296.5 12.1 %cholesky.556 = f32[128,128]{1,0:T(8,128)S(1)} custom-call(f32[128,128]{1,0:T(8,128)S(1)} %cholesky.666), custom_call_target="Cholesky" | custom-call | tf_op jit(solution)/shard_map/jit(cholesky)/cholesky | solution.py:15
  308.7 9.8 %custom-call.71 = f32[1,128,128]{1,2,0:T(8,128)S(1)} custom-call(f32[1,128,128]{2,1,0:T(8,128)S(1)} %get-tuple-element.30), custom_call_target="InvertDiagBlocksLowerTriangular" | custom-call | tf_op jit(solution)/shard_map/jit(cholesky)/cholesky | solution.py:15
  323.4 11.7 %cholesky.576 = f32[128,128]{1,0:T(8,128)S(1)} custom-call(f32[128,128]{1,0:T(8,128)S(1)} %cholesky.671), custom_call_target="Cholesky" | custom-call | tf_op jit(solution)/shard_map/jit(cholesky)/cholesky | solution.py:15
  335.2 9.8 %custom-call.72 = f32[1,128,128]{1,2,0:T(8,128)S(1)} custom-call(f32[1,128,128]{2,1,0:T(8,128)S(1)} %get-tuple-element.28), custom_call_target="InvertDiagBlocksLowerTriangular" | custom-call | tf_op jit(solution)/shard_map/jit(cholesky)/cholesky | solution.py:15
  349.5 11.7 %cholesky.596 = f32[128,128]{1,0:T(8,128)S(1)} custom-call(f32[128,128]{1,0:T(8,128)S(1)} %cholesky.676), custom_call_target="Cholesky" | custom-call | tf_op jit(solution)/shard_map/jit(cholesky)/cholesky | solution.py:15
  361.4 9.8 %custom-call.77 = f32[1,128,128]{1,2,0:T(8,128)S(1)} custom-call(f32[1,128,128]{2,1,0:T(8,128)S(1)} %get-tuple-element.26), custom_call_target="InvertDiagBlocksLowerTriangular" | custom-call | tf_op jit(solution)/shard_map/jit(cholesky)/cholesky/custom-call.17 | solution.py:15
  374.8 11.7 %cholesky.610 = f32[128,128]{1,0:T(8,128)S(1)} custom-call(f32[128,128]{1,0:T(8,128)S(1)} %convolution_subtract_fusion.8), custom_call_target="Cholesky" | custom-call | tf_op jit(solution)/shard_map/jit(cholesky)/cholesky | solution.py:15
  397.1 4.8 fusion.11
  406.9 11.7 %cholesky.623 = f32[128,128]{1,0:T(8,128)S(1)} custom-call(f32[128,128]{1,0:T(8,128)S(1)} %cholesky.680), custom_call_target="Cholesky" | custom-call | tf_op jit(solution)/shard_map/jit(cholesky)/cholesky | solution.py:28
  418.7 9.8 %custom-call.78 = f32[1,128,128]{1,2,0:T(8,128)S(1)} custom-call(f32[1,128,128]{2,1,0:T(8,128)S(1)} %get-tuple-element.24), custom_call_target="InvertDiagBlocksLowerTriangular" | custom-call | tf_op jit(solution)/shard_map/jit(cholesky)/cholesky/custom-call.17 | solution.py:28
  429.0 12.0 %cholesky.632 = f32[128,128]{1,0:T(8,128)S(1)} custom-call(f32[128,128]{1,0:T(8,128)S(1)} %convolution_subtract_fusion.7), custom_call_target="Cholesky" | custom-call | tf_op jit(solution)/shard_map/jit(cholesky)/cholesky | solution.py:28
  443.6 5.2 while.1
  448.8 20.5 %custom-call.73 = f32[2,128,128]{1,2,0:T(8,128)S(1)} custom-call(f32[2,128,128]{2,1,0:T(8,128)} %get-tuple-element.10), custom_call_target="InvertDiagBlocksLowerTriangular" | custom-call | tf_op jit(solution)/shard_map/jit(_solve_triangular)/triangular_solve | solution.py:29
  474.9 13.2 %all-to-all-start.1 = ((bf16[32,32,256]{2,1,0:T(8,128)(2,1)}), bf16[32,32,256]{2,1,0:T(8,128)(2,1)}, u32[]{:S(2)}, u32[]{:S(2)}) async-start(bf16[32,32,256]{2,1,0:T(8,128)(2,1)} %bitcast.109), calls=%async_computation.1 | async-start | bytes 1048576 | tf_op jit(solution)/shard_map/all_to_all | solution.py:52
  490.7 31.0 %all-to-all-done.1 = bf16[32,32,256]{2,1,0:T(8,128)(2,1)} async-done(((bf16[32,32,256]{2,1,0:T(8,128)(2,1)}), bf16[32,32,256]{2,1,0:T(8,128)(2,1)}, u32[]{:S(2)}, u32[]{:S(2)}) %all-to-all-start.1) | async-done | bytes 524320 | tf_op jit(solution)/shard_map/all_to_all | solution.py:52
  (105 shorter events, 62.7 us)
Async XLA Ops:
  7.2 389.9 %copy-start = (bf16[1024,256]{1,0:T(8,128)(2,1)S(1)}, bf16[1024,256]{1,0:T(8,128)(2,1)}, u32[]{:S(2)}) copy-start(bf16[1024,256]{1,0:T(8,128)(2,1)} %param.7) | copy-start | bytes 1572868
  7.2 4.0 copy-start.5
  7.2 143.6 %all-reduce.4.cloned.1.call-start = ((), (), s32[]{:S(2)}) async-start(), calls=%async_computation.2 | async-start | bytes 8388608 | tf_op jit(solution)/shard_map/psum | solution.py:45
  12.8 389.1 %all-to-all-start = ((bf16[32,32,1024]{2,0,1:T(8,128)(2,1)}), bf16[32,32,1024]{2,0,1:T(8,128)(2,1)S(1)}, u32[]{:S(2)}, u32[]{:S(2)}) async-start(bf16[32,32,1024]{2,0,1:T(8,128)(2,1)} %bitcast.107), calls=%async_computation | async-start | bytes 4194304 | tf_op jit(solution)/shard_map/all_to_all | solution.py:50
  184.5 1.9 copy-start.1
  213.9 0.8 copy-start.6
  293.3 103.8 %copy-start.7 = (bf16[256]{0:T(256)(128)(2,1)S(1)}, bf16[256]{0:T(256)(128)(2,1)}, u32[]{:S(2)}) copy-start(bf16[256]{0:T(256)(128)(2,1)} %fusion.53) | copy-start | bytes 1540
  401.9 1.4 copy-start.2
  470.5 17.6 %copy-start.3 = (bf16[32,32,1024]{2,0,1:T(8,128)(2,1)S(1)}, bf16[32,32,1024]{2,0,1:T(8,128)(2,1)}, u32[]{:S(2)}) copy-start(bf16[32,32,1024]{2,0,1:T(8,128)(2,1)} %copy-done.2) | copy-start | bytes 6291460
  471.1 0.8 copy-start.4
  474.9 46.8 %all-to-all-start.1 = ((bf16[32,32,256]{2,1,0:T(8,128)(2,1)}), bf16[32,32,256]{2,1,0:T(8,128)(2,1)}, u32[]{:S(2)}, u32[]{:S(2)}) async-start(bf16[32,32,256]{2,1,0:T(8,128)(2,1)} %bitcast.109), calls=%async_computation.1 | async-start | bytes 1048576 | tf_op jit(solution)/shard_map/all_to_all | solution.py:52
Sparse Core Ops, SparseCore 0:
  11.4 139.3 all-reduce.3
where the time goes:
time: 535 us; the launch traced here: 531 us
  other arithmetic  235 us (44%)
  waiting for transfers between devices  151 us (28%)
  local copies, waits for them, and re-layouts  47.6 us (9%)
  matrix products  44.9 us (8%)
  starting transfers between devices  30 us (6%)
  between operations  22.6 us (4%)
    another operation x30, other arithmetic, factor(): return jnp.linalg.cholesky(held)  168 us
    psum x1, waiting for transfers between devices, local(): gram = lax.psum(partial_value, 'dp')  120 us
    another operation x7, other arithmetic, compress(): inner_lower = jnp.linalg.cholesky(inner_gram)  34.8 us
    all_to_all x1, waiting for transfers between devices, local(): lax.all_to_all(basis_rows, 'tile', split_axis=0, concat_axis=1, tiled=True)  31 us
    another operation x14, matrix products, factor(): return jnp.linalg.cholesky(held)  28 us
    another operation x3, other arithmetic, compress(): jax.scipy.linalg.solve_triangular(inner_lower, range_rows.T, lower=True)  20.5 us
    gather x1, local copies, waits for them, and re-layouts, factor(): mean_diag = jnp.mean(jnp.diagonal(gram))  17.3 us
    all_to_all x1, starting transfers between devices, local(): lax.all_to_all(weights, 'tile', split_axis=1, concat_axis=0, tiled=True)  16.8 us
  transfers between devices with their start and end apart: 3, of which 2 were waited for; matrix products, arithmetic and copies ran while one was open for 47% of the time, Pallas kernels for 0%

commit v1 on v0

v1 whole, which is shorter than its diff:
```python
import functools
import math

import jax
import jax.numpy as jnp
from jax import lax
from jax.experimental import pallas as pl
from jax.experimental.pallas import tpu as pltpu
from jax.sharding import PartitionSpec as P

DAMPING = 0.1
NB = 128
STRIP = 8
F32 = jnp.float32
BF16 = jnp.bfloat16

NT = (((1,), (1,)), ((), ()))
NN = (((1,), (0,)), ((), ()))


def dot(a, b, dims):
    return lax.dot_general(a, b, dims, preferred_element_type=F32)


def split2(x):
    hi = x.astype(BF16)
    lo = (x - hi.astype(F32)).astype(BF16)
    return hi, lo


def split3(x):
    hi = x.astype(BF16)
    rest = x - hi.astype(F32)
    mid = rest.astype(BF16)
    lo = (rest - mid.astype(F32)).astype(BF16)
    return hi, mid, lo


def dot3(a, b, dims):
    ah, al = split2(a)
    bh, bl = split2(b)
    return dot(ah, bh, dims) + (dot(ah, bl, dims) + dot(al, bh, dims))


def dot6(a, b, dims):
    ah, am, al = split3(a)
    bh, bm, bl = split3(b)
    small = dot(am, bm, dims) + (dot(ah, bl, dims) + dot(al, bh, dims))
    return dot(ah, bh, dims) + ((dot(ah, bm, dims) + dot(am, bh, dims)) + small)


def recip(x):
    r = pl.reciprocal(x, approx=True)
    r = r * (2.0 - x * r)
    return r * (2.0 - x * r)


def inverse_factor(rows):
    shape = rows[0].shape
    lane = lax.broadcasted_iota(jnp.int32, shape, 1)
    sub = lax.broadcasted_iota(jnp.int32, shape, 0)
    rows = list(rows)
    out = []
    for s in range(len(rows)):
        base = s * STRIP
        strip = rows[s]
        cols = [jnp.broadcast_to(strip[:, base + k : base + k + 1], shape) for k in range(STRIP)]
        a = [
            [jnp.broadcast_to(cols[k][i : i + 1, :], shape) if i >= k else None for k in range(STRIP)]
            for i in range(STRIP)
        ]
        own = (lane >= base) & (lane < base + STRIP)
        held = jnp.where(own, jnp.where(lane - base == sub, 1.0, 0.0), strip)
        y = [jnp.broadcast_to(held[k : k + 1, :], shape) for k in range(STRIP)]
        z = []
        low = [[None] * STRIP for _ in range(STRIP)]
        done = jnp.zeros(shape, F32)
        for k in range(STRIP):
            r = recip(a[k][k])
            for i in range(k + 1, STRIP):
                low[i][k] = a[i][k] * r
            for i in range(k + 1, STRIP):
                for j in range(k + 1, i + 1):
                    a[i][j] = a[i][j] - low[i][k] * a[j][k]
                y[i] = y[i] - low[i][k] * y[k]
            z.append(y[k] * r)
            done = jnp.where(sub == k, y[k] * lax.rsqrt(a[k][k]), done)
        out.append(jnp.where(lane < base + STRIP, done, 0.0))
        if s + 1 == len(rows):
            break
        for k in range(STRIP - 1, -1, -1):
            for i in range(k):
                z[i] = z[i] - low[k][i] * z[k]
        for t in range(s + 1, len(rows)):
            low_t = rows[t]
            total = jnp.where(own, 0.0, low_t)
            for k in range(STRIP - 1, -1, -1):
                total = total - jnp.broadcast_to(low_t[:, base + k : base + k + 1], shape) * z[k]
            rows[t] = total
    return out


def load_strips(ref, index, start):
    return [ref[index, pl.ds(start + s * STRIP, STRIP), :] for s in range(NB // STRIP)]


def turn_kernel(x_ref, out_ref):
    out_ref[...] = x_ref[...].T


def turn(x):
    return pl.pallas_call(
        turn_kernel,
        out_shape=jax.ShapeDtypeStruct((x.shape[1], x.shape[0]), x.dtype),
        in_specs=[pl.BlockSpec(memory_space=pltpu.VMEM)],
        out_specs=pl.BlockSpec(memory_space=pltpu.VMEM),
    )(x)


def whiten_kernel(x_ref, sketch_ref, out_ref, a_ref, hl_ref, rr_ref, rl_ref, acc_ref, inv_ref):
    width = x_ref.shape[1]
    panels = width // NB
    chunks = x_ref.shape[0]
    wide = 2 * NB
    for c in range(panels // 2):
        lo = c * wide
        total = None
        for d in range(0, chunks, 2):
            left = jnp.concatenate([x_ref[d, lo:, :], x_ref[d + 1, lo:, :]], axis=1)
            term = dot(left, left[:wide, :], NT)
            total = term if total is None else total + term
        a_ref[2 * c, lo:, :] = total[:, :NB]
        a_ref[2 * c + 1, lo:, :] = total[:, NB:]

    lane = lax.broadcasted_iota(jnp.int32, (NB, NB), 1)
    sub = lax.broadcasted_iota(jnp.int32, (NB, NB), 0)
    diag = lane == sub
    trace = jnp.zeros((NB, NB), F32)
    for c in range(panels):
        trace = trace + jnp.where(diag, a_ref[c, c * NB : (c + 1) * NB, :], 0.0)
    damp = jnp.sum(trace) * (DAMPING / width)
    for c in range(panels):
        block = a_ref[c, c * NB : (c + 1) * NB, :]
        a_ref[c, c * NB : (c + 1) * NB, :] = jnp.where(diag, block + damp, block)

    hl_ref[...] = jnp.zeros_like(hl_ref)
    rr_ref[...] = jnp.zeros_like(rr_ref)
    rl_ref[...] = jnp.zeros_like(rl_ref)
    acc_ref[...] = jnp.zeros_like(acc_ref)

    tall_row = lax.broadcasted_iota(jnp.int32, (width, NB), 0)
    tall_lane = lax.broadcasted_iota(jnp.int32, (width, NB), 1)

    def sketch_in(p):
        part = sketch_ref[p]
        acc_ref[...] += dot(jnp.concatenate([part, part], axis=1), hl_ref[...], NT)

    def step(p, carry):
        start = pl.multiple_of(p * NB, NB)
        strips = load_strips(a_ref, p, start)
        for c in range(panels // 2):
            lo = c * wide
            both = hl_ref[lo:, :]
            off = dot(both, rr_ref[lo : lo + wide, :], NT) + dot(both[:, :NB], rl_ref[lo : lo + wide, :], NT)
            a_ref[2 * c, lo:, :] -= off[:, :NB]
            a_ref[2 * c + 1, lo:, :] -= off[:, NB:]
        sketch_in(jnp.maximum(p - 1, 0))
        for s, rows in enumerate(inverse_factor(strips)):
            inv_ref[s * STRIP : (s + 1) * STRIP, :] = rows
        ih, il = split2(inv_ref[...])
        ph, plow = split2(a_ref[p])
        panel = dot(jnp.concatenate([ph, plow], axis=1), jnp.concatenate([ih, ih], axis=1), NT) + dot(ph, il, NT)
        panel = jnp.where(tall_row >= tall_lane + start, panel, 0.0)
        hi, lo16 = split2(panel)
        hl_ref[:, :NB] = hi
        hl_ref[:, NB:] = lo16
        right = tall_row >= start + 2 * NB
        hi_r = jnp.where(right, panel, 0.0).astype(BF16)
        rr_ref[:, :NB] = hi_r
        rr_ref[:, NB:] = hi_r
        rl_ref[...] = jnp.where(right, panel - hi.astype(F32), 0.0).astype(BF16)
        nxt = jnp.minimum(p + 1, panels - 1)
        rows_n = pl.ds(pl.multiple_of(nxt * NB, NB), NB)
        near = hl_ref[rows_n, :]
        nh, nl = near[:, :NB], near[:, NB:]
        off = dot(jnp.concatenate([hi, lo16], axis=1), jnp.concatenate([nh, nh], axis=1), NT) + dot(hi, nl, NT)
        a_ref[nxt] = a_ref[nxt] - off
        return carry

    lax.fori_loop(0, panels, step, 0)
    sketch_in(panels - 1)
    out_ref[...] = acc_ref[...].astype(BF16)


def whiten(gathered, sketch_t):
    chunks, width, _ = gathered.shape
    panels, rmax, _ = sketch_t.shape
    return pl.pallas_call(
        whiten_kernel,
        out_shape=jax.ShapeDtypeStruct((rmax, width), BF16),
        in_specs=[pl.BlockSpec(memory_space=pltpu.VMEM)] * 2,
        out_specs=pl.BlockSpec(memory_space=pltpu.VMEM),
        scratch_shapes=[
            pltpu.VMEM((panels, width, NB), F32),
            pltpu.VMEM((width, 2 * NB), BF16),
            pltpu.VMEM((width, 2 * NB), BF16),
            pltpu.VMEM((width, NB), BF16),
            pltpu.VMEM((rmax, width), F32),
            pltpu.VMEM((NB, NB), F32),
        ],
        compiler_params=pltpu.CompilerParams(vmem_limit_bytes=40 * 1024 * 1024),
    )(gathered, sketch_t)


def basis_kernel(rank_ref, w_ref, sk_ref, turned_ref, basis_ref, t_ref, d_ref, off_ref, inv_ref):
    width = w_ref.shape[0]
    rmax = sk_ref.shape[0]
    rank = rank_ref[0, 0]
    kept = lax.broadcasted_iota(jnp.int32, sk_ref.shape, 0) < rank
    masked = jnp.where(kept, sk_ref[...].astype(F32), 0.0).astype(BF16)
    rows = dot(masked, w_ref[...], NT)
    inner = dot6(rows, rows, NT)
    sub = lax.broadcasted_iota(jnp.int32, (rmax, rmax), 0)
    lane = lax.broadcasted_iota(jnp.int32, (rmax, rmax), 1)
    inner = inner + jnp.where((sub == lane) & (sub >= rank), 1.0, 0.0)
    t_ref[0] = rows[:NB]
    t_ref[1] = rows[NB:]
    d_ref[0] = inner[:NB, :NB]
    d_ref[1] = inner[NB:, NB:]
    off_ref[...] = inner[NB:, :NB]

    def step(p, carry):
        for s, part in enumerate(inverse_factor(load_strips(d_ref, p, 0))):
            inv_ref[s * STRIP : (s + 1) * STRIP, :] = part
        inv = inv_ref[...]
        base = dot3(inv, t_ref[p], NN)
        low = dot6(off_ref[...], inv, NT)
        d_ref[1] = d_ref[1] - dot6(low, low, NT)
        t_ref[1] = t_ref[1] - dot6(low, base, NN)
        scaled = base * math.sqrt(width)
        turned_ref[p] = scaled.astype(BF16)
        basis_ref[:, pl.ds(pl.multiple_of(p * NB, NB), NB)] = scaled.T.astype(BF16)
        return carry

    lax.fori_loop(0, rmax // NB, step, 0)


def basis_of(rank, tile_block, sketched_t):
    width = tile_block.shape[0]
    rmax = sketched_t.shape[0]
    halves = rmax // NB
    return pl.pallas_call(
        basis_kernel,
        out_shape=(
            jax.ShapeDtypeStruct((halves, NB, width), BF16),
            jax.ShapeDtypeStruct((width, rmax), BF16),
        ),
        in_specs=[
            pl.BlockSpec(memory_space=pltpu.SMEM),
            pl.BlockSpec(memory_space=pltpu.VMEM),
            pl.BlockSpec(memory_space=pltpu.VMEM),
        ],
        out_specs=(pl.BlockSpec(memory_space=pltpu.VMEM),) * 2,
        scratch_shapes=[
            pltpu.VMEM((halves, NB, width), F32),
            pltpu.VMEM((halves, NB, NB), F32),
            pltpu.VMEM((NB, NB), F32),
            pltpu.VMEM((NB, NB), F32),
        ],
        compiler_params=pltpu.CompilerParams(vmem_limit_bytes=40 * 1024 * 1024),
    )(rank, tile_block, sketched_t)


def local(calibration, sketch, weights, tile_ranks):
    width = calibration.shape[1]
    rmax = sketch.shape[1]
    gathered = lax.all_gather(turn(calibration), "dp")
    sketch_t = sketch.reshape(width // NB, NB, rmax).transpose(0, 2, 1)
    tile_block = lax.all_to_all(weights, "tile", split_axis=1, concat_axis=0, tiled=True)
    sketched_t = whiten(gathered, sketch_t)
    turned, basis = basis_of(tile_ranks, tile_block, sketched_t)
    served = lax.all_to_all(basis, "tile", split_axis=0, concat_axis=1, tiled=True)
    coeffs = jnp.dot(turned.reshape(rmax, width), tile_block, preferred_element_type=F32) / math.sqrt(width)
    return (served, coeffs.astype(BF16))


def solution(mesh):
    placed = (P("dp", "tile"), P("tile", None), P(("dp", "tile"), None), P("dp", "tile"))
    return jax.shard_map(
        local,
        mesh=mesh,
        in_specs=placed,
        out_specs=(P(("dp", "tile"), None), P("dp", "tile")),
        check_vma=False,
    )
```

time: 535 us -> 234 us (0.44)
  other arithmetic: 235 us -> 0 us
  Pallas kernels: 0 us -> 79.5 us
  waiting for transfers between devices: 151 us -> 101 us
  matrix products: 44.9 us -> 1.51 us
  local copies, waits for them, and re-layouts: 47.6 us -> 6.44 us
  between operations: 22.6 us -> 14.7 us
    another operation x40 -> x0, other arithmetic: 223 us -> none  [the longest x30 168 us: factor(): return jnp.linalg.cholesky(held)]
    psum x1 -> x0, waiting for transfers between devices: 120 us -> none  [local(): gram = lax.psum(partial_value, 'dp')]
    pallas_call x0 -> x3, Pallas kernels: none -> 79.5 us  [the longest x1 60 us: whiten(): pl.pallas_call(whiten_kernel, out_shape=jax.ShapeDtypeStruct((rmax, width...]
    all_gather x0 -> x1, waiting for transfers between devices: none -> 69.2 us  [local(): gathered = lax.all_gather(turn(calibration), 'dp')]
    another operation x19 -> x0, matrix products: 30.3 us -> none  [the longest x14 28 us: factor(): return jnp.linalg.cholesky(held)]
    gather x1 -> x0, local copies, waits for them, and re-layouts: 17.3 us -> none  [factor(): mean_diag = jnp.mean(jnp.diagonal(gram))]
    another operation x34 -> x0, local copies, waits for them, and re-layouts: 14 us -> none  [the longest x25 8.76 us: factor(): return jnp.linalg.cholesky(held)]
    dot_general x5 -> x1, matrix products: 14.6 us -> 1.51 us  [local(): jnp.dot(turned.reshape(rmax, width), tile_block, preferred_element_type=F32)]
  transfers between devices with their start and end apart: 3 -> 3, of which waited for: 2 -> 2; matrix products, arithmetic and copies ran while one was open for 47% -> 1% of each run, Pallas kernels for 0% -> 26%
where the time goes in v1:
time: 234 us; the launch traced here: 233 us
  waiting for transfers between devices  101 us (43%)
  Pallas kernels  79.5 us (34%)
  starting transfers between devices  29.9 us (13%)
  between operations  14.7 us (6%)
  local copies, waits for them, and re-layouts  6.44 us (3%)
    all_gather x1, waiting for transfers between devices, local(): gathered = lax.all_gather(turn(calibration), 'dp')  69.2 us
    pallas_call x1, Pallas kernels, whiten(): pl.pallas_call(whiten_kernel, out_shape=jax.ShapeDtypeStruct((rmax, width...  60 us
    all_to_all x1, waiting for transfers between devices, local(): lax.all_to_all(basis, 'tile', split_axis=0, concat_axis=1, tiled=True)  32 us
    pallas_call x1, Pallas kernels, basis_of(): pl.pallas_call(basis_kernel, out_shape=(jax.ShapeDtypeStruct((halves, NB,...  17.7 us
    all_to_all x1, starting transfers between devices, local(): lax.all_to_all(weights, 'tile', split_axis=1, concat_axis=0, tiled=True)  16.9 us
    all_to_all x1, starting transfers between devices, local(): lax.all_to_all(basis, 'tile', split_axis=0, concat_axis=1, tiled=True)  13 us
  transfers between devices with their start and end apart: 3, of which 2 were waited for; matrix products, arithmetic and copies ran while one was open for 1% of the time, Pallas kernels for 26%

profile of v1, /device:TPU:1, one launch (start us, length us, event | category | flops | bytes accessed | tf_op | source)
XLA Modules:
  0.0 233.4 jit_solution(10503444680305754125)
XLA Ops:
  7.2 3.2 %copy.14 = bf16[4,32,8,1024]{3,2,0,1:T(8,128)(2,1)} copy(bf16[4,32,8,1024]{3,2,1,0:T(8,128)(2,1)} %bitcast.23) | data formatting | bytes 4194304 | tf_op jit(solution)/shard_map/all_to_all | solution.py:279
  10.3 0.0 copy-start.1
  10.3 16.9 %all-to-all-start = ((bf16[32,32,1024]{2,0,1:T(8,128)(2,1)}), bf16[32,32,1024]{2,0,1:T(8,128)(2,1)S(1)}, u32[]{:S(2)}, u32[]{:S(2)}) async-start(bf16[32,32,1024]{2,0,1:T(8,128)(2,1)} %bitcast.22), calls=%async_computation | async-start | bytes 4194304 | tf_op jit(solution)/shard_map/all_to_all | solution.py:279
  27.2 0.0 all-gather.3.cloned.1.call-start
  27.3 1.8 shard_map.59
  29.0 0.0 all-gather.3.cloned.1.call-update
  29.7 0.0 copy-done.1
  29.7 0.3 copy.9
  30.0 69.2 %all-gather.3.cloned.1.call-done = bf16[16384,128]{1,0:T(8,128)(2,1)} async-done(((bf16[1024,128]{1,0:T(8,128)(2,1)}), bf16[16384,128]{1,0:T(8,128)(2,1)}) %all-gather.3.cloned.1.call-update) | async-done | bytes 4194320 | tf_op jit(solution)/shard_map/all_gather | solution.py:277
  99.2 0.0 copy-start
  99.2 2.2 copy-done
  101.4 60.0 %shard_map.60.sk_ref = bf16[256,1024]{1,0:T(8,128)(2,1)S(1)} custom-call(bf16[16,1024,128]{2,1,0:T(8,128)(2,1)S(1)} %bitcast.19, bf16[8,256,128]{2,1,0:T(8,128)(2,1)S(1)} %bitcast.20), custom_call_target="tpu_custom_call" | custom-call | tf_op jit(solution)/shard_map/pallas_call | solution.py:198
  161.4 0.0 all-to-all-done
  161.4 17.7 %shard_map.61 = (bf16[2,128,1024]{2,1,0:T(8,128)(2,1)S(1)}, bf16[1024,256]{1,0:T(8,128)(2,1)}) custom-call(s32[1,1]{1,0:T(1,128)S(6)} %copy.15.rank_ref, bf16[1024,1024]{1,0:T(8,128)(2,1)S(1)} %bitcast.17, bf16[256,1024]{1,0:T(8,128)(2,1)S(1)} %shard_map.60.sk_ref), custom_call_target="tpu_custom_call" | custom-call | tf_op jit(solution)/shard_map/pallas_call | solution.py:252
  179.2 13.0 %all-to-all-start.1 = ((bf16[32,32,256]{2,1,0:T(8,128)(2,1)}), bf16[32,32,256]{2,1,0:T(8,128)(2,1)S(1)}, u32[]{:S(2)}, u32[]{:S(2)}) async-start(bf16[32,32,256]{2,1,0:T(8,128)(2,1)} %bitcast.5), calls=%async_computation.1 | async-start | bytes 1048576 | tf_op jit(solution)/shard_map/all_to_all | solution.py:282
  192.2 1.5 fusion
  193.7 32.0 %all-to-all-done.1 = bf16[32,32,256]{2,1,0:T(8,128)(2,1)S(1)} async-done(((bf16[32,32,256]{2,1,0:T(8,128)(2,1)}), bf16[32,32,256]{2,1,0:T(8,128)(2,1)S(1)}, u32[]{:S(2)}, u32[]{:S(2)}) %all-to-all-start.1) | async-done | bytes 524320 | tf_op jit(solution)/shard_map/all_to_all | solution.py:282
  225.7 0.8 copy.12
Async XLA Ops:
  10.3 19.4 %copy-start.1 = (bf16[1024,256]{1,0:T(8,128)(2,1)S(1)}, bf16[1024,256]{1,0:T(8,128)(2,1)}, u32[]{:S(2)}) copy-start(bf16[1024,256]{1,0:T(8,128)(2,1)} %param.5) | copy-start | bytes 1572868
  10.3 151.1 %all-to-all-start = ((bf16[32,32,1024]{2,0,1:T(8,128)(2,1)}), bf16[32,32,1024]{2,0,1:T(8,128)(2,1)S(1)}, u32[]{:S(2)}, u32[]{:S(2)}) async-start(bf16[32,32,1024]{2,0,1:T(8,128)(2,1)} %bitcast.22), calls=%async_computation | async-start | bytes 4194304 | tf_op jit(solution)/shard_map/all_to_all | solution.py:279
  27.2 72.0 %all-gather.3.cloned.1.call-start = ((), (), s32[]{:S(2)}) async-start(), calls=%async_computation.2 | async-start | bytes 4456448 | tf_op jit(solution)/shard_map/all_gather | solution.py:277
  99.2 2.2 copy-start
  179.2 46.5 %all-to-all-start.1 = ((bf16[32,32,256]{2,1,0:T(8,128)(2,1)}), bf16[32,32,256]{2,1,0:T(8,128)(2,1)S(1)}, u32[]{:S(2)}, u32[]{:S(2)}) async-start(bf16[32,32,256]{2,1,0:T(8,128)(2,1)} %bitcast.5), calls=%async_computation.1 | async-start | bytes 1048576 | tf_op jit(solution)/shard_map/all_to_all | solution.py:282
Sparse Core Ops, SparseCore 0:
  31.6 67.5 all-gather.2

commit v2 on v1

--- a/solution.py
+++ b/solution.py
@@ -117,20 +117,68 @@
     )(x)
 
 
-def whiten_kernel(x_ref, sketch_ref, out_ref, a_ref, hl_ref, rr_ref, rl_ref, acc_ref, inv_ref):
-    width = x_ref.shape[1]
+def neighbour(value, axis, shift, side=4):
+    pairs = []
+    for x in range(side):
+        for y in range(side):
+            to = ((x + shift) % side, y) if axis == 0 else (x, (y + shift) % side)
+            pairs.append((x * side + y, to[0] * side + to[1]))
+    return lax.ppermute(value, "dp", pairs)
+
+
+def gather_line(value, axis):
+    back = neighbour(value, axis, 1)
+    ahead = neighbour(value, axis, -1)
+    half = value.shape[0] // 2
+    far_a = neighbour(back[:half], axis, 1)
+    far_b = neighbour(ahead[half:], axis, -1)
+    return value, back, ahead, far_a, far_b
+
+
+def gather_plane(half, axis):
+    near, back, ahead, far_a, far_b = gather_line(half, axis)
+    line = jnp.stack([near, back, ahead, jnp.concatenate([far_a, far_b], axis=0)])
+    return gather_line(line, 1 - axis)
+
+
+def whiten_kernel(*refs):
+    first, second = refs[:5], refs[5:10]
+    sketch_ref, out_ref, a_ref, hl_ref, rr_ref, rl_ref, acc_ref, inv_ref = refs[10:]
+    half, _ = first[0].shape[1:]
+    width = 2 * half
     panels = width // NB
-    chunks = x_ref.shape[0]
     wide = 2 * NB
+
+    def piece(parts, group, place):
+        if group < 3:
+            return parts[group][place]
+        return parts[3 + place // 2][place % 2]
+
+    def chunk(dx, dy, upper):
+        return piece(first, dy, dx) if upper else piece(second, dx, dy)
+
     for c in range(panels // 2):
         lo = c * wide
-        total = None
-        for d in range(0, chunks, 2):
-            left = jnp.concatenate([x_ref[d, lo:, :], x_ref[d + 1, lo:, :]], axis=1)
-            term = dot(left, left[:wide, :], NT)
-            total = term if total is None else total + term
-        a_ref[2 * c, lo:, :] = total[:, :NB]
-        a_ref[2 * c + 1, lo:, :] = total[:, NB:]
+        top = bottom = None
+        for dx in range(0, 4, 2):
+            for dy in range(4):
+                low_part = jnp.concatenate([chunk(dx, dy, False), chunk(dx + 1, dy, False)], axis=1)
+                if lo < half:
+                    high_part = jnp.concatenate([chunk(dx, dy, True), chunk(dx + 1, dy, True)], axis=1)
+                    right = high_part[lo : lo + wide, :]
+                    term = dot(high_part[lo:, :], right, NT)
+                    top = term if top is None else top + term
+                    term = dot(low_part, right, NT)
+                else:
+                    at = lo - half
+                    term = dot(low_part[at:, :], low_part[at : at + wide, :], NT)
+                bottom = term if bottom is None else bottom + term
+        if lo < half:
+            a_ref[2 * c, lo:half, :] = top[:, :NB]
+            a_ref[2 * c + 1, lo:half, :] = top[:, NB:]
+        from_row = max(lo, half)
+        a_ref[2 * c, from_row:, :] = bottom[:, :NB]
+        a_ref[2 * c + 1, from_row:, :] = bottom[:, NB:]
 
     lane = lax.broadcasted_iota(jnp.int32, (NB, NB), 1)
     sub = lax.broadcasted_iota(jnp.int32, (NB, NB), 0)
@@ -192,13 +240,13 @@
     out_ref[...] = acc_ref[...].astype(BF16)
 
 
-def whiten(gathered, sketch_t):
-    chunks, width, _ = gathered.shape
+def whiten(parts, sketch_t):
+    width = 2 * parts[0].shape[1]
     panels, rmax, _ = sketch_t.shape
     return pl.pallas_call(
         whiten_kernel,
         out_shape=jax.ShapeDtypeStruct((rmax, width), BF16),
-        in_specs=[pl.BlockSpec(memory_space=pltpu.VMEM)] * 2,
+        in_specs=[pl.BlockSpec(memory_space=pltpu.VMEM)] * 11,
         out_specs=pl.BlockSpec(memory_space=pltpu.VMEM),
         scratch_shapes=[
             pltpu.VMEM((panels, width, NB), F32),
@@ -209,7 +257,7 @@
             pltpu.VMEM((NB, NB), F32),
         ],
         compiler_params=pltpu.CompilerParams(vmem_limit_bytes=40 * 1024 * 1024),
-    )(gathered, sketch_t)
+    )(*parts, sketch_t)
 
 
 def basis_kernel(rank_ref, w_ref, sk_ref, turned_ref, basis_ref, t_ref, d_ref, off_ref, inv_ref):
@@ -274,10 +322,11 @@
 def local(calibration, sketch, weights, tile_ranks):
     width = calibration.shape[1]
     rmax = sketch.shape[1]
-    gathered = lax.all_gather(turn(calibration), "dp")
+    turned_x = turn(calibration)
+    parts = gather_plane(turned_x[: width // 2], 0) + gather_plane(turned_x[width // 2 :], 1)
     sketch_t = sketch.reshape(width // NB, NB, rmax).transpose(0, 2, 1)
     tile_block = lax.all_to_all(weights, "tile", split_axis=1, concat_axis=0, tiled=True)
-    sketched_t = whiten(gathered, sketch_t)
+    sketched_t = whiten(parts, sketch_t)
     turned, basis = basis_of(tile_ranks, tile_block, sketched_t)
     served = lax.all_to_all(basis, "tile", split_axis=0, concat_axis=1, tiled=True)
     coeffs = jnp.dot(turned.reshape(rmax, width), tile_block, preferred_element_type=F32) / math.sqrt(width)

time: 234 us -> 222 us (0.949)
  waiting for transfers between devices: 101 us -> 33.9 us
  starting transfers between devices: 29.9 us -> 85.6 us
  between operations: 14.7 us -> 1.68 us
  local copies, waits for them, and re-layouts: 6.44 us -> 17.3 us
    all_gather x1 -> x0, waiting for transfers between devices: 69.2 us -> none  [local(): gathered = lax.all_gather(turn(calibration), 'dp')]
    ppermute x0 -> x16, starting transfers between devices: none -> 52 us  [neighbour(): return lax.ppermute(value, 'dp', pairs)]
    unnamed x4 -> x22, local copies, waits for them, and re-layouts: 2.19 us -> 7.06 us
    all_to_all x1, starting transfers between devices: 13 us -> 16.8 us  [local(): lax.all_to_all(basis, 'tile', split_axis=0, concat_axis=1, tiled=True)]
    slice x0 -> x8, local copies, waits for them, and re-layouts: none -> 3.14 us  [the longest x4 1.6 us: gather_line(): far_b = neighbour(ahead[half:], axis, -1)]
  transfers between devices with their start and end apart: 3 -> 18, of which waited for: 2 -> 3; matrix products, arithmetic and copies ran while one was open for 1% -> 4% of each run, Pallas kernels for 26% -> 28%
where the time goes in v2:
time: 222 us; the launch traced here: 221 us
  starting transfers between devices  85.6 us (39%)
  Pallas kernels  80.6 us (36%)
  waiting for transfers between devices  33.9 us (15%)
  local copies, waits for them, and re-layouts  17.3 us (8%)
    pallas_call x1, Pallas kernels, whiten(): pl.pallas_call(whiten_kernel, out_shape=jax.ShapeDtypeStruct((rmax, width...  61.1 us
    ppermute x16, starting transfers between devices, neighbour(): return lax.ppermute(value, 'dp', pairs)  52 us
    all_to_all x1, waiting for transfers between devices, local(): lax.all_to_all(basis, 'tile', split_axis=0, concat_axis=1, tiled=True)  32 us
    pallas_call x1, Pallas kernels, basis_of(): pl.pallas_call(basis_kernel, out_shape=(jax.ShapeDtypeStruct((halves, NB,...  17.7 us
    all_to_all x1, starting transfers between devices, local(): lax.all_to_all(basis, 'tile', split_axis=0, concat_axis=1, tiled=True)  16.8 us
    all_to_all x1, starting transfers between devices, local(): lax.all_to_all(weights, 'tile', split_axis=1, concat_axis=0, tiled=True)  16.7 us
    unnamed x22, local copies, waits for them, and re-layouts  7.06 us
  transfers between devices with their start and end apart: 18, of which 3 were waited for; matrix products, arithmetic and copies ran while one was open for 4% of the time, Pallas kernels for 28%

profile of v2, /device:TPU:1, one launch (start us, length us, event | category | flops | bytes accessed | tf_op | source)
XLA Modules:
  0.0 220.6 jit_solution(18101388054618582128)
XLA Ops:
  0.6 3.2 %copy.14 = bf16[4,32,8,1024]{3,2,0,1:T(8,128)(2,1)} copy(bf16[4,32,8,1024]{3,2,1,0:T(8,128)(2,1)} %bitcast.33) | data formatting | bytes 4194304 | tf_op jit(solution)/shard_map/all_to_all | solution.py:328
  3.8 16.7 %all-to-all-start = ((bf16[32,32,1024]{2,0,1:T(8,128)(2,1)}), bf16[32,32,1024]{2,0,1:T(8,128)(2,1)S(1)}, u32[]{:S(2)}, u32[]{:S(2)}) async-start(bf16[32,32,1024]{2,0,1:T(8,128)(2,1)} %bitcast.32), calls=%async_computation | async-start | bytes 4194304 | tf_op jit(solution)/shard_map/all_to_all | solution.py:328
  20.6 1.8 shard_map.59
  22.4 1.0 slice_bitcast_fusion
  23.4 3.2 %collective-permute-start.8 = (bf16[512,128]{1,0:T(8,128)(2,1)S(1)}, bf16[512,128]{1,0:T(8,128)(2,1)S(1)}, u32[]{:S(2)}, u32[]{:S(2)}) collective-permute-start(bf16[512,128]{1,0:T(8,128)(2,1)S(1)} %get-tuple-element.8), channel_id=1, source_target_pairs={{0,32},{32,64},{64,96},{96,0},{128,160},{160,192},{192,224},{224,1... | collective-permute-start | bytes 393224 | tf_op jit(solution)/shard_map/ppermute | solution.py:126
  26.6 3.4 %collective-permute-start.9 = (bf16[512,128]{1,0:T(8,128)(2,1)S(1)}, bf16[512,128]{1,0:T(8,128)(2,1)S(1)}, u32[]{:S(2)}, u32[]{:S(2)}) collective-permute-start(bf16[512,128]{1,0:T(8,128)(2,1)S(1)} %get-tuple-element.8), channel_id=1, source_target_pairs={{0,96},{32,0},{64,32},{96,64},{128,224},{160,128},{192,160},{224,1... | collective-permute-start | bytes 393224 | tf_op jit(solution)/shard_map/ppermute | solution.py:126
  30.0 3.1 %collective-permute-start = (bf16[512,128]{1,0:T(8,128)(2,1)S(1)}, bf16[512,128]{1,0:T(8,128)(2,1)S(1)}, u32[]{:S(2)}, u32[]{:S(2)}) collective-permute-start(bf16[512,128]{1,0:T(8,128)(2,1)S(1)} %get-tuple-element.9), channel_id=1, source_target_pairs={{0,128},{32,160},{64,192},{96,224},{128,256},{160,288},{192,320},{... | collective-permute-start | bytes 393224 | tf_op jit(solution)/shard_map/ppermute | solution.py:126
  33.1 3.4 %collective-permute-start.1 = (bf16[512,128]{1,0:T(8,128)(2,1)S(1)}, bf16[512,128]{1,0:T(8,128)(2,1)S(1)}, u32[]{:S(2)}, u32[]{:S(2)}) collective-permute-start(bf16[512,128]{1,0:T(8,128)(2,1)S(1)} %get-tuple-element.9), channel_id=1, source_target_pairs={{0,384},{32,416},{64,448},{96,480},{128,0},{160,32},{192,64},{224,... | collective-permute-start | bytes 393224 | tf_op jit(solution)/shard_map/ppermute | solution.py:126
  36.5 1.9 collective-permute-start.10
  38.5 4.6 %collective-permute-start.11 = (bf16[256,128]{1,0:T(8,128)(2,1)S(1)}, bf16[256,128]{1,0:T(8,128)(2,1)S(1)}, u32[]{:S(2)}, u32[]{:S(2)}) collective-permute-start(bf16[256,128]{1,0:T(8,128)(2,1)S(1)} %slice.47), channel_id=1, source_target_pairs={{0,96},{32,0},{64,32},{96,64},{128,224},{160,128},{192,160},{224,1... | collective-permute-start | bytes 196616 | tf_op jit(solution)/shard_map/ppermute | solution.py:126
  43.1 1.9 collective-permute-start.2
  45.0 4.6 %collective-permute-start.3 = (bf16[256,128]{1,0:T(8,128)(2,1)S(1)}, bf16[256,128]{1,0:T(8,128)(2,1)S(1)}, u32[]{:S(2)}, u32[]{:S(2)}) collective-permute-start(bf16[256,128]{1,0:T(8,128)(2,1)S(1)} %slice.42), channel_id=1, source_target_pairs={{0,384},{32,416},{64,448},{96,480},{128,0},{160,32},{192,64},{224,... | collective-permute-start | bytes 196616 | tf_op jit(solution)/shard_map/ppermute | solution.py:126
  49.7 1.9 collective-permute-start.12
  51.6 4.6 %collective-permute-start.13 = (bf16[4,512,128]{2,1,0:T(8,128)(2,1)S(1)}, bf16[4,512,128]{2,1,0:T(8,128)(2,1)S(1)}, u32[]{:S(2)}, u32[]{:S(2)}) collective-permute-start(bf16[4,512,128]{2,1,0:T(8,128)(2,1)S(1)} %pad_maximum_fusion.1.refs_5_), channel_id=1, source_target_pairs={{0,384},{32,416},{64,448},{96,480},{128,0},{160,32},{192,64},{224,... | collective-permute-start | bytes 1572872 | tf_op jit(solution)/shard_map/ppermute | solution.py:126
  56.3 1.9 collective-permute-start.4
  58.3 4.6 %collective-permute-start.5 = (bf16[4,512,128]{2,1,0:T(8,128)(2,1)S(1)}, bf16[4,512,128]{2,1,0:T(8,128)(2,1)S(1)}, u32[]{:S(2)}, u32[]{:S(2)}) collective-permute-start(bf16[4,512,128]{2,1,0:T(8,128)(2,1)S(1)} %pad_maximum_fusion.refs_0_), channel_id=1, source_target_pairs={{0,96},{32,0},{64,32},{96,64},{128,224},{160,128},{192,160},{224,1... | collective-permute-start | bytes 1572872 | tf_op jit(solution)/shard_map/ppermute | solution.py:126
  64.6 1.9 collective-permute-start.14
  67.3 4.6 %collective-permute-start.15 = (bf16[2,512,128]{2,1,0:T(8,128)(2,1)}, bf16[2,512,128]{2,1,0:T(8,128)(2,1)}, u32[]{:S(2)}, u32[]{:S(2)}) collective-permute-start(bf16[2,512,128]{2,1,0:T(8,128)(2,1)} %slice.49), channel_id=1, source_target_pairs={{0,384},{32,416},{64,448},{96,480},{128,0},{160,32},{192,64},{224,... | collective-permute-start | bytes 786440 | tf_op jit(solution)/shard_map/ppermute | solution.py:126
  72.7 1.9 collective-permute-start.6
  75.4 4.6 %collective-permute-start.7 = (bf16[2,512,128]{2,1,0:T(8,128)(2,1)}, bf16[2,512,128]{2,1,0:T(8,128)(2,1)}, u32[]{:S(2)}, u32[]{:S(2)}) collective-permute-start(bf16[2,512,128]{2,1,0:T(8,128)(2,1)} %slice.44), channel_id=1, source_target_pairs={{0,96},{32,0},{64,32},{96,64},{128,224},{160,128},{192,160},{224,1... | collective-permute-start | bytes 786440 | tf_op jit(solution)/shard_map/ppermute | solution.py:126
  80.0 2.1 copy.9
  83.6 1.0 copy-done
  84.7 1.0 copy-done.4
  85.7 1.0 copy-done.6
  86.7 1.0 copy-done.8
  87.8 1.0 copy-done.10
  88.8 61.1 %shard_map.60.sk_ref = bf16[256,1024]{1,0:T(8,128)(2,1)S(1)} custom-call(bf16[4,512,128]{2,1,0:T(8,128)(2,1)S(1)} %pad_maximum_fusion.refs_0_, bf16[4,512,128]{2,1,0:T(8,128)(2,1)S(1)} %copy-done.8, bf16[4,512,128]{2,1,0:T(8,128)(2,1)S(1)} %copy-done.10, bf16[2,512,128]{2,1,0:T(8,128)(2,1)} %collective-permute-done.6.refs_3_, ...), custom_call_target="tpu_custom_call" | custom-call | tf_op jit(solution)/shard_map/pallas_call | solution.py:246
  150.7 1.0 copy-done.2
  151.7 17.7 %shard_map.61 = (bf16[2,128,1024]{2,1,0:T(8,128)(2,1)S(1)}, bf16[1024,256]{1,0:T(8,128)(2,1)}) custom-call(s32[1,1]{1,0:T(1,128)S(6)} %copy.15.rank_ref, bf16[1024,1024]{1,0:T(8,128)(2,1)S(1)} %bitcast.28, bf16[256,1024]{1,0:T(8,128)(2,1)S(1)} %copy-done.2), custom_call_target="tpu_custom_call" | custom-call | tf_op jit(solution)/shard_map/pallas_call | solution.py:300
  169.5 16.8 %all-to-all-start.1 = ((bf16[32,32,256]{2,1,0:T(8,128)(2,1)}), bf16[32,32,256]{2,1,0:T(8,128)(2,1)S(1)}, u32[]{:S(2)}, u32[]{:S(2)}) async-start(bf16[32,32,256]{2,1,0:T(8,128)(2,1)} %bitcast.12), calls=%async_computation.1 | async-start | bytes 1048576 | tf_op jit(solution)/shard_map/all_to_all | solution.py:331
  186.3 1.5 fusion
  187.8 32.0 %all-to-all-done.1 = bf16[32,32,256]{2,1,0:T(8,128)(2,1)S(1)} async-done(((bf16[32,32,256]{2,1,0:T(8,128)(2,1)}), bf16[32,32,256]{2,1,0:T(8,128)(2,1)S(1)}, u32[]{:S(2)}, u32[]{:S(2)}) %all-to-all-start.1) | async-done | bytes 524320 | tf_op jit(solution)/shard_map/all_to_all | solution.py:331
  (46 shorter events, 6.8 us)
Async XLA Ops:
  3.8 146.9 %all-to-all-start = ((bf16[32,32,1024]{2,0,1:T(8,128)(2,1)}), bf16[32,32,1024]{2,0,1:T(8,128)(2,1)S(1)}, u32[]{:S(2)}, u32[]{:S(2)}) async-start(bf16[32,32,1024]{2,0,1:T(8,128)(2,1)} %bitcast.32), calls=%async_computation | async-start | bytes 4194304 | tf_op jit(solution)/shard_map/all_to_all | solution.py:328
  23.4 13.1 %collective-permute-start.8 = (bf16[512,128]{1,0:T(8,128)(2,1)S(1)}, bf16[512,128]{1,0:T(8,128)(2,1)S(1)}, u32[]{:S(2)}, u32[]{:S(2)}) collective-permute-start(bf16[512,128]{1,0:T(8,128)(2,1)S(1)} %get-tuple-element.8), channel_id=1, source_target_pairs={{0,32},{32,64},{64,96},{96,0},{128,160},{160,192},{192,224},{224,1... | collective-permute-start | bytes 393224 | tf_op jit(solution)/shard_map/ppermute | solution.py:126
  26.6 11.8 %collective-permute-start.9 = (bf16[512,128]{1,0:T(8,128)(2,1)S(1)}, bf16[512,128]{1,0:T(8,128)(2,1)S(1)}, u32[]{:S(2)}, u32[]{:S(2)}) collective-permute-start(bf16[512,128]{1,0:T(8,128)(2,1)S(1)} %get-tuple-element.8), channel_id=1, source_target_pairs={{0,96},{32,0},{64,32},{96,64},{128,224},{160,128},{192,160},{224,1... | collective-permute-start | bytes 393224 | tf_op jit(solution)/shard_map/ppermute | solution.py:126
  30.0 13.1 %collective-permute-start = (bf16[512,128]{1,0:T(8,128)(2,1)S(1)}, bf16[512,128]{1,0:T(8,128)(2,1)S(1)}, u32[]{:S(2)}, u32[]{:S(2)}) collective-permute-start(bf16[512,128]{1,0:T(8,128)(2,1)S(1)} %get-tuple-element.9), channel_id=1, source_target_pairs={{0,128},{32,160},{64,192},{96,224},{128,256},{160,288},{192,320},{... | collective-permute-start | bytes 393224 | tf_op jit(solution)/shard_map/ppermute | solution.py:126
  33.1 11.9 %collective-permute-start.1 = (bf16[512,128]{1,0:T(8,128)(2,1)S(1)}, bf16[512,128]{1,0:T(8,128)(2,1)S(1)}, u32[]{:S(2)}, u32[]{:S(2)}) collective-permute-start(bf16[512,128]{1,0:T(8,128)(2,1)S(1)} %get-tuple-element.9), channel_id=1, source_target_pairs={{0,384},{32,416},{64,448},{96,480},{128,0},{160,32},{192,64},{224,... | collective-permute-start | bytes 393224 | tf_op jit(solution)/shard_map/ppermute | solution.py:126
  36.5 13.1 %collective-permute-start.10 = (bf16[256,128]{1,0:T(8,128)(2,1)S(1)}, bf16[256,128]{1,0:T(8,128)(2,1)S(1)}, u32[]{:S(2)}, u32[]{:S(2)}) collective-permute-start(bf16[256,128]{1,0:T(8,128)(2,1)S(1)} %slice.46), channel_id=1, source_target_pairs={{0,32},{32,64},{64,96},{96,0},{128,160},{160,192},{192,224},{224,1... | collective-permute-start | bytes 196616 | tf_op jit(solution)/shard_map/ppermute | solution.py:126
  38.5 11.1 %collective-permute-start.11 = (bf16[256,128]{1,0:T(8,128)(2,1)S(1)}, bf16[256,128]{1,0:T(8,128)(2,1)S(1)}, u32[]{:S(2)}, u32[]{:S(2)}) collective-permute-start(bf16[256,128]{1,0:T(8,128)(2,1)S(1)} %slice.47), channel_id=1, source_target_pairs={{0,96},{32,0},{64,32},{96,64},{128,224},{160,128},{192,160},{224,1... | collective-permute-start | bytes 196616 | tf_op jit(solution)/shard_map/ppermute | solution.py:126
  43.1 13.2 %collective-permute-start.2 = (bf16[256,128]{1,0:T(8,128)(2,1)S(1)}, bf16[256,128]{1,0:T(8,128)(2,1)S(1)}, u32[]{:S(2)}, u32[]{:S(2)}) collective-permute-start(bf16[256,128]{1,0:T(8,128)(2,1)S(1)} %slice.41), channel_id=1, source_target_pairs={{0,128},{32,160},{64,192},{96,224},{128,256},{160,288},{192,320},{... | collective-permute-start | bytes 196616 | tf_op jit(solution)/shard_map/ppermute | solution.py:126
  45.0 11.2 %collective-permute-start.3 = (bf16[256,128]{1,0:T(8,128)(2,1)S(1)}, bf16[256,128]{1,0:T(8,128)(2,1)S(1)}, u32[]{:S(2)}, u32[]{:S(2)}) collective-permute-start(bf16[256,128]{1,0:T(8,128)(2,1)S(1)} %slice.42), channel_id=1, source_target_pairs={{0,384},{32,416},{64,448},{96,480},{128,0},{160,32},{192,64},{224,... | collective-permute-start | bytes 196616 | tf_op jit(solution)/shard_map/ppermute | solution.py:126
  49.7 14.1 %collective-permute-start.12 = (bf16[4,512,128]{2,1,0:T(8,128)(2,1)S(1)}, bf16[4,512,128]{2,1,0:T(8,128)(2,1)S(1)}, u32[]{:S(2)}, u32[]{:S(2)}) collective-permute-start(bf16[4,512,128]{2,1,0:T(8,128)(2,1)S(1)} %pad_maximum_fusion.1.refs_5_), channel_id=1, source_target_pairs={{0,128},{32,160},{64,192},{96,224},{128,256},{160,288},{192,320},{... | collective-permute-start | bytes 1572872 | tf_op jit(solution)/shard_map/ppermute | solution.py:126
  51.6 14.9 %collective-permute-start.13 = (bf16[4,512,128]{2,1,0:T(8,128)(2,1)S(1)}, bf16[4,512,128]{2,1,0:T(8,128)(2,1)S(1)}, u32[]{:S(2)}, u32[]{:S(2)}) collective-permute-start(bf16[4,512,128]{2,1,0:T(8,128)(2,1)S(1)} %pad_maximum_fusion.1.refs_5_), channel_id=1, source_target_pairs={{0,384},{32,416},{64,448},{96,480},{128,0},{160,32},{192,64},{224,... | collective-permute-start | bytes 1572872 | tf_op jit(solution)/shard_map/ppermute | solution.py:126
  56.3 15.6 %collective-permute-start.4 = (bf16[4,512,128]{2,1,0:T(8,128)(2,1)S(1)}, bf16[4,512,128]{2,1,0:T(8,128)(2,1)S(1)}, u32[]{:S(2)}, u32[]{:S(2)}) collective-permute-start(bf16[4,512,128]{2,1,0:T(8,128)(2,1)S(1)} %pad_maximum_fusion.refs_0_), channel_id=1, source_target_pairs={{0,32},{32,64},{64,96},{96,0},{128,160},{160,192},{192,224},{224,1... | collective-permute-start | bytes 1572872 | tf_op jit(solution)/shard_map/ppermute | solution.py:126
  58.3 16.4 %collective-permute-start.5 = (bf16[4,512,128]{2,1,0:T(8,128)(2,1)S(1)}, bf16[4,512,128]{2,1,0:T(8,128)(2,1)S(1)}, u32[]{:S(2)}, u32[]{:S(2)}) collective-permute-start(bf16[4,512,128]{2,1,0:T(8,128)(2,1)S(1)} %pad_maximum_fusion.refs_0_), channel_id=1, source_target_pairs={{0,96},{32,0},{64,32},{96,64},{128,224},{160,128},{192,160},{224,1... | collective-permute-start | bytes 1572872 | tf_op jit(solution)/shard_map/ppermute | solution.py:126
  63.8 10.8 %copy-start.3 = (bf16[4,512,128]{2,1,0:T(8,128)(2,1)}, bf16[4,512,128]{2,1,0:T(8,128)(2,1)S(1)}, u32[]{:S(2)}) copy-start(bf16[4,512,128]{2,1,0:T(8,128)(2,1)S(1)} %collective-permute-done.12.refs_6_) | copy-start | bytes 1572868
  64.6 18.1 %collective-permute-start.14 = (bf16[2,512,128]{2,1,0:T(8,128)(2,1)}, bf16[2,512,128]{2,1,0:T(8,128)(2,1)S(1)}, u32[]{:S(2)}, u32[]{:S(2)}) collective-permute-start(bf16[2,512,128]{2,1,0:T(8,128)(2,1)} %slice.48), channel_id=1, source_target_pairs={{0,128},{32,160},{64,192},{96,224},{128,256},{160,288},{192,320},{... | collective-permute-start | bytes 786440 | tf_op jit(solution)/shard_map/ppermute | solution.py:126
  66.5 8.9 %copy-start.5 = (bf16[4,512,128]{2,1,0:T(8,128)(2,1)}, bf16[4,512,128]{2,1,0:T(8,128)(2,1)S(1)}, u32[]{:S(2)}) copy-start(bf16[4,512,128]{2,1,0:T(8,128)(2,1)S(1)} %collective-permute-done.13.refs_7_) | copy-start | bytes 1572868
  67.3 15.4 %collective-permute-start.15 = (bf16[2,512,128]{2,1,0:T(8,128)(2,1)}, bf16[2,512,128]{2,1,0:T(8,128)(2,1)}, u32[]{:S(2)}, u32[]{:S(2)}) collective-permute-start(bf16[2,512,128]{2,1,0:T(8,128)(2,1)} %slice.49), channel_id=1, source_target_pairs={{0,384},{32,416},{64,448},{96,480},{128,0},{160,32},{192,64},{224,... | collective-permute-start | bytes 786440 | tf_op jit(solution)/shard_map/ppermute | solution.py:126
  71.9 8.1 %copy-start.7 = (bf16[4,512,128]{2,1,0:T(8,128)(2,1)}, bf16[4,512,128]{2,1,0:T(8,128)(2,1)S(1)}, u32[]{:S(2)}) copy-start(bf16[4,512,128]{2,1,0:T(8,128)(2,1)S(1)} %collective-permute-done.4.refs_1_) | copy-start | bytes 1572868
  72.7 10.1 %collective-permute-start.6 = (bf16[2,512,128]{2,1,0:T(8,128)(2,1)}, bf16[2,512,128]{2,1,0:T(8,128)(2,1)}, u32[]{:S(2)}, u32[]{:S(2)}) collective-permute-start(bf16[2,512,128]{2,1,0:T(8,128)(2,1)} %slice.43), channel_id=1, source_target_pairs={{0,32},{32,64},{64,96},{96,0},{128,160},{160,192},{192,224},{224,1... | collective-permute-start | bytes 786440 | tf_op jit(solution)/shard_map/ppermute | solution.py:126
  74.6 5.4 %copy-start.9 = (bf16[4,512,128]{2,1,0:T(8,128)(2,1)}, bf16[4,512,128]{2,1,0:T(8,128)(2,1)S(1)}, u32[]{:S(2)}) copy-start(bf16[4,512,128]{2,1,0:T(8,128)(2,1)S(1)} %collective-permute-done.5.refs_2_) | copy-start | bytes 1572868
  75.4 8.2 %collective-permute-start.7 = (bf16[2,512,128]{2,1,0:T(8,128)(2,1)}, bf16[2,512,128]{2,1,0:T(8,128)(2,1)}, u32[]{:S(2)}, u32[]{:S(2)}) collective-permute-start(bf16[2,512,128]{2,1,0:T(8,128)(2,1)} %slice.44), channel_id=1, source_target_pairs={{0,96},{32,0},{64,32},{96,64},{128,224},{160,128},{192,160},{224,1... | collective-permute-start | bytes 786440 | tf_op jit(solution)/shard_map/ppermute | solution.py:126
  83.6 1.0 copy-start
  84.7 1.0 copy-start.4
  85.7 1.0 copy-start.6
  86.7 1.0 copy-start.8
  87.8 1.0 copy-start.10
  149.9 0.8 copy-start.1
  150.7 1.0 copy-start.2
  169.5 50.4 %all-to-all-start.1 = ((bf16[32,32,256]{2,1,0:T(8,128)(2,1)}), bf16[32,32,256]{2,1,0:T(8,128)(2,1)S(1)}, u32[]{:S(2)}, u32[]{:S(2)}) async-start(bf16[32,32,256]{2,1,0:T(8,128)(2,1)} %bitcast.12), calls=%async_computation.1 | async-start | bytes 1048576 | tf_op jit(solution)/shard_map/all_to_all | solution.py:331
